TPU v7x, 768 devices: a whole 4x8x12 slice. The times are simulated.
768 devices in a mesh: ctx: 96 (over y_lo, z, core), head: 8 (over y_hi, x).
Axes of the slice: x: 4, y: 8 (y_hi: 2, y_lo: 4; y = y_hi * 4 + y_lo), z: 12, core: 2. Of those that a mesh axis runs over, the one named last changes fastest.
Arguments:
- queries: bfloat16 [24576, 5120], P('ctx', 'head'), may hold values from -6 to 6
- keys: bfloat16 [24576, 1024], P('ctx', 'head'), may hold values from -6 to 6
- values: bfloat16 [24576, 1024], P('ctx', 'head'), may hold values from -6 to 6
- segment_ids: int32 [24576], P('ctx'), may hold values from 0 to 191, never falling along the last dimension, each value on 1 to 1280 neighbouring positions
- out_weight: bfloat16 [5120, 5120], P('head'), may hold values from -0.078125 to 0.078125
Outputs:
- projected: bfloat16 [24576, 5120], P('ctx', 'head')
Inputs may be any that keep to these rules, and one draw needn't show every extreme that they name: `segment_ids`: ids never fall along the tokens; each document holds 1 to 6 - 1 times 256 tokens, one exactly that many; every id of 0 to 191 is used.
All inputs are finite; a program needn't handle non-finite values.
Results may differ from a plain program's by a relative error of at most 0.019.
Values may be sent and summed in bfloat16 or wider, within the bound.
A program may use at most 32 MiB of HBM per device.

v0:
```python
import jax
import jax.numpy as jnp
from jax import lax
from jax.sharding import PartitionSpec as P

HD = 128
SPAN = 6


def passed_along(block, axis, distance):
    devices = range(lax.axis_size(axis))
    route = [(i - distance, i) for i in devices if i - distance in devices]
    return lax.ppermute(block, axis, route)


def shards(queries, keys, values, segment_ids, out_weight):
    rows_here = queries.shape[0]
    query_width = queries.shape[1]
    kv_width = keys.shape[1]
    kv_count = kv_width // HD
    sharing = query_width // kv_width
    scaling = 1.0 / HD**0.5
    my_index = lax.axis_index("ctx")
    query_pos = my_index * rows_here + jnp.arange(rows_here, dtype=jnp.int32)
    query_rows = queries.reshape(rows_here, kv_count, sharing, HD)

    def absorb(carry, key_block, val_block, seg_block, key_pos):
        peak, total, accum = carry
        scores = (
            jnp.einsum(
                "qgrd,kgd->grqk",
                query_rows,
                key_block.reshape(rows_here, kv_count, HD),
                preferred_element_type=jnp.float32,
            )
            * scaling
        )
        allowed = (
            (segment_ids[:, None] == seg_block[None, :])
            & (key_pos[None, :] <= query_pos[:, None])
            & (key_pos[None, :] >= 0)
        )
        scores = jnp.where(allowed[None, None], scores, -1e30)
        new_peak = jnp.maximum(peak, jnp.max(scores, axis=-1))
        factor = jnp.exp(peak - new_peak)
        expo = jnp.exp(scores - new_peak[..., None])
        total = total * factor + jnp.sum(expo, axis=-1)
        weights = expo.astype(jnp.bfloat16)
        accum = accum * factor[..., None] + jnp.einsum(
            "grqk,kgd->grqd",
            weights,
            val_block.reshape(rows_here, kv_count, HD),
            preferred_element_type=jnp.float32,
        )
        return (new_peak, total, accum)

    carry = (
        jnp.full((kv_count, sharing, rows_here), -1e30, jnp.float32),
        jnp.zeros((kv_count, sharing, rows_here), jnp.float32),
        jnp.zeros((kv_count, sharing, rows_here, HD), jnp.float32),
    )
    carry = absorb(carry, keys, values, segment_ids, query_pos)
    previous = (keys, values, segment_ids)
    for distance in range(1, SPAN):
        arrived = passed_along((previous[0], previous[1], previous[2]), "ctx", 1)
        previous = arrived
        key_block, val_block, seg_block = arrived
        key_pos = (my_index - distance) * rows_here + jnp.arange(rows_here, dtype=jnp.int32)
        carry = absorb(carry, key_block, val_block, seg_block, key_pos)
    peak, total, accum = carry
    attended = (accum / total[..., None]).astype(jnp.bfloat16)
    attended = jnp.transpose(attended, (2, 0, 1, 3)).reshape(rows_here, query_width)
    partial_term = jnp.dot(attended, out_weight, preferred_element_type=jnp.float32)
    return lax.psum_scatter(
        partial_term.astype(jnp.bfloat16), "head", scatter_dimension=1, tiled=True
    )


def solution(mesh):
    in_specs = (P("ctx", "head"), P("ctx", "head"), P("ctx", "head"), P("ctx"), P("head", None))
    out_specs = P("ctx", "head")
    return jax.shard_map(shards, mesh=mesh, in_specs=in_specs, out_specs=out_specs, check_vma=False)
```

profile of v0, /device:TPU:1, one launch (start us, length us, event | category | flops | bytes accessed | tf_op | source)
XLA Modules:
  0.0 209.9 jit_solution(14823075725431617592)
XLA Ops:
  6.5 5.4 %collective-permute-start = (s32[256]{0:T(256)}, s32[256]{0:T(256)S(1)}, u32[]{:S(2)}, u32[]{:S(2)}) collective-permute-start(s32[256]{0:T(256)} %param.8), channel_id=1, source_target_pairs={{0,8},{8,16},{16,24},{24,32},{32,40},{40,48},{48,56},{56,64},{64,7... | collective-permute-start | bytes 3080 | tf_op jit(solution)/shard_map/ppermute | solution.py:13
  11.9 1.9 collective-permute-start.1
  14.8 4.4 %collective-permute-start.2 = (bf16[256,128]{0,1:T(8,128)(2,1)S(1)}, bf16[256,128]{0,1:T(8,128)(2,1)S(1)}, u32[]{:S(2)}, u32[]{:S(2)}) collective-permute-start(bf16[256,128]{0,1:T(8,128)(2,1)S(1)} %copy.40), channel_id=1, source_target_pairs={{0,8},{8,16},{16,24},{24,32},{32,40},{40,48},{48,56},{56,64},{64,7... | collective-permute-start | bytes 196616 | tf_op jit(solution)/shard_map/ppermute | solution.py:13
  19.3 1.9 collective-permute-start.3
  21.3 2.7 %collective-permute-done.3 = s32[256]{0:T(256)S(1)} collective-permute-done((s32[256]{0:T(256)S(1)}, s32[256]{0:T(256)S(1)}, u32[]{:S(2)}, u32[]{:S(2)}) %collective-permute-start.3) | collective-permute-done | bytes 1056 | tf_op jit(solution)/shard_map/ppermute | solution.py:13
  23.9 2.5 %collective-permute-start.6 = (s32[256]{0:T(256)S(1)}, s32[256]{0:T(256)S(1)}, u32[]{:S(2)}, u32[]{:S(2)}) collective-permute-start(s32[256]{0:T(256)S(1)} %collective-permute-done.3), channel_id=1, source_target_pairs={{0,8},{8,16},{16,24},{24,32},{32,40},{40,48},{48,56},{56,64},{64,7... | collective-permute-start | bytes 3080 | tf_op jit(solution)/shard_map/ppermute | solution.py:13
  27.1 4.2 %collective-permute-start.9 = (s32[256]{0:T(256)S(1)}, s32[256]{0:T(256)S(1)}, u32[]{:S(2)}, u32[]{:S(2)}) collective-permute-start(s32[256]{0:T(256)S(1)} %collective-permute-done.6), channel_id=1, source_target_pairs={{0,8},{8,16},{16,24},{24,32},{32,40},{40,48},{48,56},{56,64},{64,7... | collective-permute-start | bytes 3080 | tf_op jit(solution)/shard_map/ppermute | solution.py:13
  32.0 4.2 %collective-permute-start.12 = (s32[256]{0:T(256)S(1)}, s32[256]{0:T(256)S(1)}, u32[]{:S(2)}, u32[]{:S(2)}) collective-permute-start(s32[256]{0:T(256)S(1)} %collective-permute-done.9), channel_id=1, source_target_pairs={{0,8},{8,16},{16,24},{24,32},{32,40},{40,48},{48,56},{56,64},{64,7... | collective-permute-start | bytes 3080 | tf_op jit(solution)/shard_map/ppermute | solution.py:13
  36.2 1.1 copy.35
  37.4 1.7 and_and_fusion.4
  39.1 1.2 fusion.74
  40.3 3.7 %collective-permute-start.4 = (bf16[256,128]{1,0:T(8,128)(2,1)S(1)}, bf16[256,128]{1,0:T(8,128)(2,1)S(1)}, u32[]{:S(2)}, u32[]{:S(2)}) collective-permute-start(bf16[256,128]{1,0:T(8,128)(2,1)S(1)} %collective-permute-done.1), channel_id=1, source_target_pairs={{0,8},{8,16},{16,24},{24,32},{32,40},{40,48},{48,56},{56,64},{64,7... | collective-permute-start | bytes 196616 | tf_op jit(solution)/shard_map/ppermute | solution.py:13
  44.4 3.9 %collective-permute-start.5 = (bf16[256,128]{0,1:T(8,128)(2,1)S(1)}, bf16[256,128]{0,1:T(8,128)(2,1)S(1)}, u32[]{:S(2)}, u32[]{:S(2)}) collective-permute-start(bf16[256,128]{0,1:T(8,128)(2,1)S(1)} %collective-permute-done.2), channel_id=1, source_target_pairs={{0,8},{8,16},{16,24},{24,32},{32,40},{40,48},{48,56},{56,64},{64,7... | collective-permute-start | bytes 196616 | tf_op jit(solution)/shard_map/ppermute | solution.py:13
  48.2 3.7 %collective-permute-start.7 = (bf16[256,128]{1,0:T(8,128)(2,1)S(1)}, bf16[256,128]{1,0:T(8,128)(2,1)S(1)}, u32[]{:S(2)}, u32[]{:S(2)}) collective-permute-start(bf16[256,128]{1,0:T(8,128)(2,1)S(1)} %collective-permute-done.4), channel_id=1, source_target_pairs={{0,8},{8,16},{16,24},{24,32},{32,40},{40,48},{48,56},{56,64},{64,7... | collective-permute-start | bytes 196616 | tf_op jit(solution)/shard_map/ppermute | solution.py:13
  52.3 2.6 %collective-permute-start.8 = (bf16[256,128]{0,1:T(8,128)(2,1)S(1)}, bf16[256,128]{0,1:T(8,128)(2,1)S(1)}, u32[]{:S(2)}, u32[]{:S(2)}) collective-permute-start(bf16[256,128]{0,1:T(8,128)(2,1)S(1)} %collective-permute-done.5), channel_id=1, source_target_pairs={{0,8},{8,16},{16,24},{24,32},{32,40},{40,48},{48,56},{56,64},{64,7... | collective-permute-start | bytes 196616 | tf_op jit(solution)/shard_map/ppermute | solution.py:13
  54.9 4.3 %collective-permute-start.10 = (bf16[256,128]{1,0:T(8,128)(2,1)S(1)}, bf16[256,128]{1,0:T(8,128)(2,1)S(1)}, u32[]{:S(2)}, u32[]{:S(2)}) collective-permute-start(bf16[256,128]{1,0:T(8,128)(2,1)S(1)} %collective-permute-done.7), channel_id=1, source_target_pairs={{0,8},{8,16},{16,24},{24,32},{32,40},{40,48},{48,56},{56,64},{64,7... | collective-permute-start | bytes 196616 | tf_op jit(solution)/shard_map/ppermute | solution.py:13
  59.5 5.4 %collective-permute-start.11 = (bf16[256,128]{0,1:T(8,128)(2,1)S(1)}, bf16[256,128]{0,1:T(8,128)(2,1)S(1)}, u32[]{:S(2)}, u32[]{:S(2)}) collective-permute-start(bf16[256,128]{0,1:T(8,128)(2,1)S(1)} %collective-permute-done.8), channel_id=1, source_target_pairs={{0,8},{8,16},{16,24},{24,32},{32,40},{40,48},{48,56},{56,64},{64,7... | collective-permute-start | bytes 196616 | tf_op jit(solution)/shard_map/ppermute | solution.py:13
  64.9 4.9 %collective-permute-start.13 = (bf16[256,128]{1,0:T(8,128)(2,1)S(1)}, bf16[256,128]{1,0:T(8,128)(2,1)S(1)}, u32[]{:S(2)}, u32[]{:S(2)}) collective-permute-start(bf16[256,128]{1,0:T(8,128)(2,1)S(1)} %collective-permute-done.10), channel_id=1, source_target_pairs={{0,8},{8,16},{16,24},{24,32},{32,40},{40,48},{48,56},{56,64},{64,7... | collective-permute-start | bytes 196616 | tf_op jit(solution)/shard_map/ppermute | solution.py:13
  70.2 1.9 collective-permute-start.14
  76.9 1.0 slice-done.1
  77.9 2.2 %convolution_convert_fusion = bf16[256,5120]{1,0:T(8,128)(2,1)S(1)} fusion(bf16[256,640]{0,1:T(8,128)(2,1)S(1)} %bitcast.117, bf16[640,5120]{1,0:T(8,128)(2,1)S(1)} %bitcast.116), kind=kOutput, calls=%fused_computation | convolution fusion | flops 1679032320 | bytes 9502720 | tf_op jit(solution)/shard_map/dot_general | solution.py:73
  80.1 2.6 %copy.64 = bf16[256,5120]{0,1:T(8,128)(2,1)} copy(bf16[256,5120]{1,0:T(8,128)(2,1)S(1)} %convolution_convert_fusion) | data formatting | bytes 5242880
  82.7 118.5 %reduce-scatter.4.cloned.1.call-done = bf16[640,256]{1,0:T(8,128)(2,1)} async-done(((bf16[5120,256]{1,0:T(8,128)(2,1)}), bf16[640,256]{1,0:T(8,128)(2,1)}) %reduce-scatter.4.cloned.1.call-update) | async-done | bytes 327696
  201.2 1.9 copy.65
  (51 shorter events, 8.5 us)
Async XLA Ops:
  6.5 194.6 %reduce-scatter.4.cloned.1.call-start = ((), (), s32[]{:S(2)}) async-start(), calls=%async_computation.1 | async-start | bytes 2949120
  6.5 12.8 %collective-permute-start = (s32[256]{0:T(256)}, s32[256]{0:T(256)S(1)}, u32[]{:S(2)}, u32[]{:S(2)}) collective-permute-start(s32[256]{0:T(256)} %param.8), channel_id=1, source_target_pairs={{0,8},{8,16},{16,24},{24,32},{32,40},{40,48},{48,56},{56,64},{64,7... | collective-permute-start | bytes 3080 | tf_op jit(solution)/shard_map/ppermute | solution.py:13
  11.9 28.4 %collective-permute-start.1 = (bf16[256,128]{1,0:T(8,128)(2,1)}, bf16[256,128]{1,0:T(8,128)(2,1)S(1)}, u32[]{:S(2)}, u32[]{:S(2)}) collective-permute-start(bf16[256,128]{1,0:T(8,128)(2,1)} %param.6), channel_id=1, source_target_pairs={{0,8},{8,16},{16,24},{24,32},{32,40},{40,48},{48,56},{56,64},{64,7... | collective-permute-start | bytes 196616 | tf_op jit(solution)/shard_map/ppermute | solution.py:13
  14.8 29.5 %collective-permute-start.2 = (bf16[256,128]{0,1:T(8,128)(2,1)S(1)}, bf16[256,128]{0,1:T(8,128)(2,1)S(1)}, u32[]{:S(2)}, u32[]{:S(2)}) collective-permute-start(bf16[256,128]{0,1:T(8,128)(2,1)S(1)} %copy.40), channel_id=1, source_target_pairs={{0,8},{8,16},{16,24},{24,32},{32,40},{40,48},{48,56},{56,64},{64,7... | collective-permute-start | bytes 196616 | tf_op jit(solution)/shard_map/ppermute | solution.py:13
  19.3 4.6 %collective-permute-start.3 = (s32[256]{0:T(256)S(1)}, s32[256]{0:T(256)S(1)}, u32[]{:S(2)}, u32[]{:S(2)}) collective-permute-start(s32[256]{0:T(256)S(1)} %collective-permute-done), channel_id=1, source_target_pairs={{0,8},{8,16},{16,24},{24,32},{32,40},{40,48},{48,56},{56,64},{64,7... | collective-permute-start | bytes 3080 | tf_op jit(solution)/shard_map/ppermute | solution.py:13
  23.9 3.2 %collective-permute-start.6 = (s32[256]{0:T(256)S(1)}, s32[256]{0:T(256)S(1)}, u32[]{:S(2)}, u32[]{:S(2)}) collective-permute-start(s32[256]{0:T(256)S(1)} %collective-permute-done.3), channel_id=1, source_target_pairs={{0,8},{8,16},{16,24},{24,32},{32,40},{40,48},{48,56},{56,64},{64,7... | collective-permute-start | bytes 3080 | tf_op jit(solution)/shard_map/ppermute | solution.py:13
  27.1 4.9 %collective-permute-start.9 = (s32[256]{0:T(256)S(1)}, s32[256]{0:T(256)S(1)}, u32[]{:S(2)}, u32[]{:S(2)}) collective-permute-start(s32[256]{0:T(256)S(1)} %collective-permute-done.6), channel_id=1, source_target_pairs={{0,8},{8,16},{16,24},{24,32},{32,40},{40,48},{48,56},{56,64},{64,7... | collective-permute-start | bytes 3080 | tf_op jit(solution)/shard_map/ppermute | solution.py:13
  32.0 5.3 %collective-permute-start.12 = (s32[256]{0:T(256)S(1)}, s32[256]{0:T(256)S(1)}, u32[]{:S(2)}, u32[]{:S(2)}) collective-permute-start(s32[256]{0:T(256)S(1)} %collective-permute-done.9), channel_id=1, source_target_pairs={{0,8},{8,16},{16,24},{24,32},{32,40},{40,48},{48,56},{56,64},{64,7... | collective-permute-start | bytes 3080 | tf_op jit(solution)/shard_map/ppermute | solution.py:13
  40.3 7.9 %collective-permute-start.4 = (bf16[256,128]{1,0:T(8,128)(2,1)S(1)}, bf16[256,128]{1,0:T(8,128)(2,1)S(1)}, u32[]{:S(2)}, u32[]{:S(2)}) collective-permute-start(bf16[256,128]{1,0:T(8,128)(2,1)S(1)} %collective-permute-done.1), channel_id=1, source_target_pairs={{0,8},{8,16},{16,24},{24,32},{32,40},{40,48},{48,56},{56,64},{64,7... | collective-permute-start | bytes 196616 | tf_op jit(solution)/shard_map/ppermute | solution.py:13
  44.4 7.9 %collective-permute-start.5 = (bf16[256,128]{0,1:T(8,128)(2,1)S(1)}, bf16[256,128]{0,1:T(8,128)(2,1)S(1)}, u32[]{:S(2)}, u32[]{:S(2)}) collective-permute-start(bf16[256,128]{0,1:T(8,128)(2,1)S(1)} %collective-permute-done.2), channel_id=1, source_target_pairs={{0,8},{8,16},{16,24},{24,32},{32,40},{40,48},{48,56},{56,64},{64,7... | collective-permute-start | bytes 196616 | tf_op jit(solution)/shard_map/ppermute | solution.py:13
  48.2 6.7 %collective-permute-start.7 = (bf16[256,128]{1,0:T(8,128)(2,1)S(1)}, bf16[256,128]{1,0:T(8,128)(2,1)S(1)}, u32[]{:S(2)}, u32[]{:S(2)}) collective-permute-start(bf16[256,128]{1,0:T(8,128)(2,1)S(1)} %collective-permute-done.4), channel_id=1, source_target_pairs={{0,8},{8,16},{16,24},{24,32},{32,40},{40,48},{48,56},{56,64},{64,7... | collective-permute-start | bytes 196616 | tf_op jit(solution)/shard_map/ppermute | solution.py:13
  52.3 7.3 %collective-permute-start.8 = (bf16[256,128]{0,1:T(8,128)(2,1)S(1)}, bf16[256,128]{0,1:T(8,128)(2,1)S(1)}, u32[]{:S(2)}, u32[]{:S(2)}) collective-permute-start(bf16[256,128]{0,1:T(8,128)(2,1)S(1)} %collective-permute-done.5), channel_id=1, source_target_pairs={{0,8},{8,16},{16,24},{24,32},{32,40},{40,48},{48,56},{56,64},{64,7... | collective-permute-start | bytes 196616 | tf_op jit(solution)/shard_map/ppermute | solution.py:13
  54.9 10.0 %collective-permute-start.10 = (bf16[256,128]{1,0:T(8,128)(2,1)S(1)}, bf16[256,128]{1,0:T(8,128)(2,1)S(1)}, u32[]{:S(2)}, u32[]{:S(2)}) collective-permute-start(bf16[256,128]{1,0:T(8,128)(2,1)S(1)} %collective-permute-done.7), channel_id=1, source_target_pairs={{0,8},{8,16},{16,24},{24,32},{32,40},{40,48},{48,56},{56,64},{64,7... | collective-permute-start | bytes 196616 | tf_op jit(solution)/shard_map/ppermute | solution.py:13
  59.5 10.7 %collective-permute-start.11 = (bf16[256,128]{0,1:T(8,128)(2,1)S(1)}, bf16[256,128]{0,1:T(8,128)(2,1)S(1)}, u32[]{:S(2)}, u32[]{:S(2)}) collective-permute-start(bf16[256,128]{0,1:T(8,128)(2,1)S(1)} %collective-permute-done.8), channel_id=1, source_target_pairs={{0,8},{8,16},{16,24},{24,32},{32,40},{40,48},{48,56},{56,64},{64,7... | collective-permute-start | bytes 196616 | tf_op jit(solution)/shard_map/ppermute | solution.py:13
  64.9 7.2 %collective-permute-start.13 = (bf16[256,128]{1,0:T(8,128)(2,1)S(1)}, bf16[256,128]{1,0:T(8,128)(2,1)S(1)}, u32[]{:S(2)}, u32[]{:S(2)}) collective-permute-start(bf16[256,128]{1,0:T(8,128)(2,1)S(1)} %collective-permute-done.10), channel_id=1, source_target_pairs={{0,8},{8,16},{16,24},{24,32},{32,40},{40,48},{48,56},{56,64},{64,7... | collective-permute-start | bytes 196616 | tf_op jit(solution)/shard_map/ppermute | solution.py:13
  70.2 6.2 %collective-permute-start.14 = (bf16[256,128]{0,1:T(8,128)(2,1)S(1)}, bf16[256,128]{0,1:T(8,128)(2,1)S(1)}, u32[]{:S(2)}, u32[]{:S(2)}) collective-permute-start(bf16[256,128]{0,1:T(8,128)(2,1)S(1)} %collective-permute-done.11), channel_id=1, source_target_pairs={{0,8},{8,16},{16,24},{24,32},{32,40},{40,48},{48,56},{56,64},{64,7... | collective-permute-start | bytes 196616 | tf_op jit(solution)/shard_map/ppermute | solution.py:13
  73.5 0.8 copy-start
  74.7 2.2 %slice-start = ((s8[6553600]{0:T(1024)(128)(4,1)}), s8[4194304]{0:T(1024)(128)(4,1)S(1)}, s32[]{:S(2)}) async-start(s8[6553600]{0:T(1024)(128)(4,1)} %bitcast.115), calls=%async_computation.2 | async-start | bytes 8388608
  75.6 2.3 %slice-start.1 = ((s8[6553600]{0:T(1024)(128)(4,1)}), s8[2359296]{0:T(1024)(128)(4,1)S(1)}, s32[]{:S(2)}) async-start(s8[6553600]{0:T(1024)(128)(4,1)} %bitcast.115), calls=%async_computation.3 | async-start | bytes 4718592
Sparse Core Ops, SparseCore 0:
  82.8 118.2 reduce-scatter.3
where the time goes:
time: 211 us; the launch traced here: 210 us
  waiting for transfers between devices  123 us (58%)
  starting transfers between devices  54.7 us (26%)
  between operations  13.9 us (7%)
  local copies, waits for them, and re-layouts  7.9 us (4%)
  matrix products  7.62 us (4%)
  other arithmetic  3.23 us (2%)
    unnamed x2, waiting for transfers between devices  118 us
    ppermute x15, starting transfers between devices, passed_along(): return lax.ppermute(block, axis, route)  54.7 us
    unnamed x10, local copies, waits for them, and re-layouts  7.9 us
  transfers between devices with their start and end apart: 16, of which 4 were waited for; matrix products, arithmetic and copies ran while one was open for 5% of the time, Pallas kernels for 0%

commit v1 on v0

v1 whole, which is shorter than its diff:
```python
import functools
import math

import jax
import jax.numpy as jnp
from jax import lax
from jax.experimental import pallas as pl
from jax.experimental.pallas import tpu as pltpu
from jax.sharding import PartitionSpec as P

HD = 128
SPAN = 6
ROWS = 256
SEGROWS = 16
NX = 4
HALF = ROWS // 2
SUB = 128
NSUB = 5
MESH = pl.DeviceIdType.MESH
NEG = -1e30


def kernel(
    chips, share,
    q_hbm, k_hbm, v_hbm, s_hbm, w_hbm, out,
    q_v, kx, vv, seg_v, w_v, acc, att,
    s1, r1, keep, s2, r2, s3, r3,
    load_sem, ks_sem, kr_sem, vs_sem, vr_sem, fs_sem, fr_sem,
):
    ctx = lax.axis_index("ctx")
    head = lax.axis_index("head")
    chip, core = ctx // 2, ctx % 2
    yh, x = head // NX, head % NX
    x1 = x + 1 - 2 * (x % 2)
    x3 = NX - 1 - x
    xo = (x + 2) % NX
    nxt, prv = (chip + 1) % chips, (chip + chips - 1) % chips
    dev_x1 = (ctx, yh * NX + x1)
    dev_x3 = (ctx, yh * NX + x3)
    dev_y = (ctx, (1 - yh) * NX + x)
    dev_sib = (chip * 2 + 1 - core, head)
    dev_next = (nxt * 2 + core, head)

    barrier = pltpu.get_barrier_semaphore()
    for device in (dev_y, dev_x1, dev_x3, dev_sib, (prv * 2 + core, head)):
        pl.semaphore_signal(barrier, inc=1, device_id=device, device_id_type=MESH)

    @pl.when(core == 0)
    def _():
        pl.semaphore_signal(barrier, inc=1, device_id=(prv * 2 + 1, head), device_id_type=MESH)

    loads = [
        pltpu.make_async_copy(s_hbm, seg_v, load_sem.at[0]),
        pltpu.make_async_copy(k_hbm, kx.at[0, pl.ds(0, ROWS)], load_sem.at[1]),
        pltpu.make_async_copy(v_hbm, vv.at[0], load_sem.at[2]),
        pltpu.make_async_copy(q_hbm, q_v, load_sem.at[3]),
        pltpu.make_async_copy(w_hbm, w_v, load_sem.at[4]),
    ]
    for load in loads:
        load.start()

    for d in range(1, SPAN):
        @pl.when(ctx < d)
        def _():
            kx[d, 0:ROWS, :] = jnp.zeros((ROWS, HD), jnp.bfloat16)
            kx[d, ROWS:, :] = jnp.full((SEGROWS, HD), -1.0, jnp.bfloat16)
            vv[d] = jnp.zeros((ROWS, HD), jnp.bfloat16)

    loads[0].wait()
    seg = seg_v[...].astype(jnp.float32)
    seg_lo, seg_hi = seg[:, :HD], seg[:, HD:]
    line = lax.broadcasted_iota(jnp.int32, (SEGROWS, HD), 0)
    both = jnp.where(line == 0, jnp.broadcast_to(seg_lo, (SEGROWS, HD)), jnp.broadcast_to(seg_hi, (SEGROWS, HD)))
    kx[0, ROWS:, :] = both.astype(jnp.bfloat16)
    first = jnp.min(seg, axis=1, keepdims=True)
    loads[1].wait()
    loads[2].wait()
    pl.semaphore_wait(barrier, 5 + core)

    def k_copy(index, slot, to_slot, device):
        return pltpu.make_async_remote_copy(
            src_ref=kx.at[slot], dst_ref=kx.at[to_slot],
            send_sem=ks_sem.at[index], recv_sem=kr_sem.at[to_slot],
            device_id=device, device_id_type=MESH)

    def v_copy(index, slot, to_slot, device):
        return pltpu.make_async_remote_copy(
            src_ref=vv.at[slot], dst_ref=vv.at[to_slot],
            send_sem=vs_sem.at[index], recv_sem=vr_sem.at[to_slot],
            device_id=device, device_id_type=MESH)

    plan = [
        (0, 2, dev_next, chip < chips - 1),
        (0, 1, dev_sib, core == 0),
        (2, 4, dev_next, (chip >= 1) & (chip < chips - 1)),
        (2, 3 - 2 * core, dev_sib, chip >= 1),
        (4, 5, (nxt * 2, head), (chip >= 2) & (chip < chips - 1) & (core == 1)),
        (4, 5 - 2 * core, dev_sib, chip >= 2),
    ]

    def send(make, slot):
        for index, (source, target, device, cond) in enumerate(plan):
            if source == slot:
                @pl.when(cond)
                def _():
                    make(index, source, target, device).start()

    def arrive(make, slot):
        @pl.when(ctx >= slot)
        def _():
            make(0, slot, slot, dev_next).wait_recv()

    send(k_copy, 0)
    send(v_copy, 0)
    loads[3].wait()

    scale = math.log2(math.e) / math.sqrt(HD)
    key_row = lax.broadcasted_iota(jnp.int32, (ROWS, ROWS), 0)
    peaks, totals = [None] * share, [None] * share

    def absorb(slot, allowed):
        vt = vv[slot].T
        for h in range(share):
            scores = lax.dot_general(
                kx[slot, 0:ROWS, :], q_v[:, h * HD:(h + 1) * HD],
                (((1,), (1,)), ((), ())), preferred_element_type=jnp.float32)
            scores = jnp.where(allowed, scores, NEG)
            top = jnp.max(scores, axis=0, keepdims=True)
            if slot > 0:
                top = jnp.maximum(top, peaks[h])
            expo = jnp.exp2((scores - top) * scale)
            total = jnp.sum(expo, axis=0, keepdims=True)
            part = jnp.dot(vt, expo.astype(jnp.bfloat16), preferred_element_type=jnp.float32)
            if slot > 0:
                factor = jnp.exp2((peaks[h] - top) * scale)
                total = total + totals[h] * factor
                part = part + acc[h] * factor
            peaks[h], totals[h] = top, total
            if slot < SPAN - 1:
                acc[h] = part
            else:
                att[:, h * HD:(h + 1) * HD] = (part / total).T.astype(jnp.bfloat16)

    seg_col = jnp.concatenate(
        [jnp.broadcast_to(seg_lo, (HD, HD)).T, jnp.broadcast_to(seg_hi, (HD, HD)).T], axis=0)
    seg_col = jnp.concatenate([seg_col, seg_col], axis=1)
    query_col = lax.broadcasted_iota(jnp.int32, (ROWS, ROWS), 1)
    absorb(0, (seg_col == seg) & (key_row <= query_col))
    for slot in (2, 1, 4, 3, 5):
        arrive(k_copy, slot)
        send(k_copy, slot)
        arrive(v_copy, slot)
        send(v_copy, slot)
        ids = kx[slot, ROWS:, :].astype(jnp.float32)
        same = jnp.where((line < 2) & (ids == first), 1.0, 0.0)
        count = jnp.sum(jnp.sum(same, axis=0, keepdims=True), axis=1, keepdims=True)
        start = jnp.where(seg == first, ROWS - count, float(ROWS)).astype(jnp.int32)
        absorb(slot, key_row >= start)

    loads[4].wait()

    pairs = ((dev_x1, dev_x3), (dev_x3, dev_x1))

    def column(xx, yi, j):
        yy = yh if yi == 0 else 1 - yh
        return pl.ds(pl.multiple_of((yy * NX + xx) * (SUB * NSUB) + j * SUB, SUB), SUB)

    def product(xs, j):
        weights = jnp.concatenate([w_v[:, column(xx, yi, j)] for xx in xs for yi in range(2)], axis=1)
        return jnp.dot(att[...], weights, preferred_element_type=jnp.float32)

    def s1_copy(j, side):
        return pltpu.make_async_remote_copy(
            src_ref=s1.at[j, side], dst_ref=r1.at[j, side],
            send_sem=fs_sem.at[0, j, side], recv_sem=fr_sem.at[0, j, side],
            device_id=pairs[side][0], device_id_type=MESH)

    def s2_copy(j, side):
        return pltpu.make_async_remote_copy(
            src_ref=s2.at[j, side], dst_ref=r2.at[j, side],
            send_sem=fs_sem.at[1, j, side], recv_sem=fr_sem.at[1, j, side],
            device_id=pairs[side][1], device_id_type=MESH)

    def s3_copy(j, side):
        return pltpu.make_async_remote_copy(
            src_ref=s3.at[j, side], dst_ref=r3.at[j, side],
            send_sem=fs_sem.at[2, j, side], recv_sem=fr_sem.at[2, j, side],
            device_id=dev_y, device_id_type=MESH)

    def stage1(j):
        p = product((x1, xo), j)
        for b in range(4):
            piece = p[:, b * SUB:(b + 1) * SUB]
            s1[j, 0, b] = piece[:HALF].astype(jnp.bfloat16)
            if b < 2:
                keep[j, 1, 2 + b] = piece[HALF:]
            else:
                s1[j, 1, b] = piece[HALF:].astype(jnp.bfloat16)
        s1_copy(j, 0).start()
        p = product((x3, x), j)
        for b in range(4):
            piece = p[:, b * SUB:(b + 1) * SUB]
            if b < 2:
                s1[j, 1, b] = piece[HALF:].astype(jnp.bfloat16)
                keep[j, 0, 2 + b] = piece[:HALF]
            else:
                keep[j, 0, b - 2] = piece[:HALF]
                keep[j, 1, b - 2] = piece[HALF:]
        s1_copy(j, 1).start()

    def stage2(j):
        for side in range(2):
            s1_copy(j, side).wait_recv()
            for b in range(2):
                s2[j, side, b] = (keep[j, side, 2 + b] + r1[j, side, 2 + b].astype(jnp.float32)).astype(jnp.bfloat16)
            s2_copy(j, side).start()
            for b in range(2):
                keep[j, side, b] = keep[j, side, b] + r1[j, side, b].astype(jnp.float32)

    def stage3(j):
        for side in range(2):
            s2_copy(j, side).wait_recv()
            s3[j, side] = (keep[j, side, 1] + r2[j, side, 1].astype(jnp.float32)).astype(jnp.bfloat16)
            s3_copy(j, side).start()
            keep[j, side, 0] = keep[j, side, 0] + r2[j, side, 0].astype(jnp.float32)

    def finish(j):
        for side in range(2):
            s3_copy(j, side).wait_recv()
            out[side * HALF:(side + 1) * HALF, j * SUB:(j + 1) * SUB] = (
                keep[j, side, 0] + r3[j, side].astype(jnp.float32)).astype(jnp.bfloat16)

    stage1(0)
    stage1(1)
    for j in range(NSUB):
        stage2(j)
        if j + 2 < NSUB:
            stage1(j + 2)
        if j >= 1:
            stage3(j - 1)
        if j >= 3:
            finish(j - 3)
    stage3(NSUB - 1)
    for j in range(NSUB - 3, NSUB):
        finish(j)

    for j in range(NSUB):
        for side in range(2):
            s1_copy(j, side).wait_send()
            s2_copy(j, side).wait_send()
            s3_copy(j, side).wait_send()
    for make in (k_copy, v_copy):
        for index, (source, target, device, cond) in enumerate(plan):
            @pl.when(cond)
            def _():
                make(index, source, target, device).wait_send()


def solution(mesh):
    chips = mesh.shape["ctx"] // 2

    def shards(queries, keys, values, segment_ids, out_weight):
        share = queries.shape[1] // HD
        cols = out_weight.shape[1] // mesh.shape["head"]
        bf, f32 = jnp.bfloat16, jnp.float32
        return pl.pallas_call(
            functools.partial(kernel, chips, share),
            name="attend_project",
            out_shape=jax.ShapeDtypeStruct((ROWS, cols), bf),
            in_specs=[pl.BlockSpec(memory_space=pl.ANY)] * 5,
            out_specs=pl.BlockSpec(memory_space=pltpu.VMEM),
            scratch_shapes=[
                pltpu.VMEM(queries.shape, bf),
                pltpu.VMEM((SPAN, ROWS + SEGROWS, HD), bf),
                pltpu.VMEM((SPAN, ROWS, HD), bf),
                pltpu.VMEM((1, ROWS), jnp.int32),
                pltpu.VMEM(out_weight.shape, bf),
                pltpu.VMEM((share, HD, ROWS), f32),
                pltpu.VMEM(queries.shape, bf),
                pltpu.VMEM((NSUB, 2, 4, HALF, SUB), bf),
                pltpu.VMEM((NSUB, 2, 4, HALF, SUB), bf),
                pltpu.VMEM((NSUB, 2, 4, HALF, SUB), f32),
                pltpu.VMEM((NSUB, 2, 2, HALF, SUB), bf),
                pltpu.VMEM((NSUB, 2, 2, HALF, SUB), bf),
                pltpu.VMEM((NSUB, 2, HALF, SUB), bf),
                pltpu.VMEM((NSUB, 2, HALF, SUB), bf),
                pltpu.SemaphoreType.DMA((5,)),
                pltpu.SemaphoreType.DMA((SPAN,)),
                pltpu.SemaphoreType.DMA((SPAN,)),
                pltpu.SemaphoreType.DMA((SPAN,)),
                pltpu.SemaphoreType.DMA((SPAN,)),
                pltpu.SemaphoreType.DMA((3, NSUB, 2)),
                pltpu.SemaphoreType.DMA((3, NSUB, 2)),
            ],
            compiler_params=pltpu.CompilerParams(
                collective_id=0, has_side_effects=True, vmem_limit_bytes=60 * 2**20),
        )(queries, keys, values, segment_ids.reshape(1, ROWS), out_weight)

    in_specs = (P("ctx", "head"), P("ctx", "head"), P("ctx", "head"), P("ctx"), P("head", None))
    return jax.shard_map(shards, mesh=mesh, in_specs=in_specs, out_specs=P("ctx", "head"), check_vma=False)
```

time: 211 us -> 64.8 us (0.31)
  the two profiles are of different devices: /device:TPU:1 before, /device:TPU:8 now
where the time goes in v1:
time: 64.8 us; the launch traced here: 64.7 us
  Pallas kernels  62.9 us (97%)
  local copies, waits for them, and re-layouts  1.73 us (3%)
    pallas_call x1, Pallas kernels, shards(): pl.pallas_call(functools.partial(kernel, chips, share), name='attend_proj...  62.9 us
    unnamed x1, local copies, waits for them, and re-layouts  1.73 us

profile of v1, /device:TPU:8, one launch (start us, length us, event | category | flops | bytes accessed | tf_op | source)
XLA Modules:
  0.0 64.7 jit_solution(5531637866571556839)
XLA Ops:
  0.0 62.9 %attend_project.1 = bf16[256,640]{1,0:T(8,128)(2,1)} custom-call(bf16[256,640]{1,0:T(8,128)(2,1)} %q_hbm.1, bf16[256,128]{1,0:T(8,128)(2,1)} %k_hbm.1, bf16[256,128]{1,0:T(8,128)(2,1)} %v_hbm.1, s32[1,256]{1,0:T(1,128)} %bitcast.1, bf16[640,5120]{1,0:T(8,128)(2,1)} %w_hbm.1), custom_call_target="tpu_custom_call" | custom-call | tf_op jit(solution)/shard_map/attend_project/pallas_call | solution.py:266
  62.9 1.7 %copy.7 = bf16[256,640]{1,0:T(8,128)(2,1)} copy(bf16[256,640]{1,0:T(8,128)(2,1)} %attend_project.1) | data formatting | bytes 655360

commit v2 on v1

v2 whole, which is shorter than its diff:
```python
import functools
import math

import jax
import jax.numpy as jnp
from jax import lax
from jax.experimental import pallas as pl
from jax.experimental.pallas import tpu as pltpu
from jax.sharding import PartitionSpec as P

HD = 128
SPAN = 6
ROWS = 256
SEGROWS = 16
NX = 4
NZ = 12
BLOCK = 640
PARTS = (((0, 384, 0), (0, 256, 384)), ((384, 256, 0), (256, 384, 256)))
CHUNKS = ((0, 64), (64, 64), (128, 64), (192, 64))
NCH = len(CHUNKS)
MESH = pl.DeviceIdType.MESH
NEG = -1e30
LANES = 128


def kernel(
    chips, share,
    q_hbm, k_hbm, v_hbm, s_hbm, w_hbm, out,
    q_v, kx, vv, seg_v, wx, acc, att, attx, own, s2, r2, res, s3, r3,
    load_sem, ks_sem, kr_sem, vs_sem, vr_sem, ws_sem, wr_sem, as_sem, ar_sem, fs_sem, fr_sem,
):
    ctx = lax.axis_index("ctx")
    head = lax.axis_index("head")
    chip, core = ctx // 2, ctx % 2
    yh, x = head // NX, head % NX
    x1 = x + 1 - 2 * (x % 2)
    x3 = NX - 1 - x
    xo = (x + 2) % NX
    nxt, prv = (chip + 1) % chips, (chip + chips - 1) % chips
    dev_x1 = (ctx, yh * NX + x1)
    dev_x3 = (ctx, yh * NX + x3)
    dev_y = (ctx, (1 - yh) * NX + x)
    dev_sib = (chip * 2 + 1 - core, head)
    dev_next = (nxt * 2 + core, head)

    barrier = pltpu.get_barrier_semaphore()
    for device in (dev_y, dev_x1, dev_x3, dev_sib, (prv * 2 + core, head)):
        pl.semaphore_signal(barrier, inc=1, device_id=device, device_id_type=MESH)

    @pl.when(core == 0)
    def _():
        pl.semaphore_signal(barrier, inc=1, device_id=(prv * 2 + 1, head), device_id_type=MESH)

    depth = w_hbm.shape[0]
    dests = ((x, x3), (x, x1))
    partner = ((dev_x1, x1, xo), (dev_x3, x3, xo))

    def span(xx, yy, side):
        first, width, _ = PARTS[side][yy]
        return pl.ds(pl.multiple_of((yy * NX + xx) * BLOCK + first, HD), width)

    def spot(d, yy, side):
        return pl.ds(d * BLOCK + PARTS[side][yy][2], PARTS[side][yy][1])

    part = depth // 2
    mine = pl.ds(pl.multiple_of(core * part, 16), part)
    theirs = pl.ds(pl.multiple_of(depth + core * part, 16), part)
    others = pl.ds(pl.multiple_of(depth + (1 - core) * part, 16), part)
    loads = [
        pltpu.make_async_copy(s_hbm, seg_v, load_sem.at[0]),
        pltpu.make_async_copy(k_hbm, kx.at[0, pl.ds(0, ROWS)], load_sem.at[1]),
        pltpu.make_async_copy(v_hbm, vv.at[0], load_sem.at[2]),
        pltpu.make_async_copy(q_hbm, q_v, load_sem.at[3]),
    ]
    w_sends = []
    for side in range(2):
        for d in range(2):
            for yy in range(2):
                n = (side * 2 + d) * 2 + yy
                loads.append(pltpu.make_async_copy(
                    w_hbm.at[:, span(dests[side][d], yy, side)],
                    wx.at[side, pl.ds(0, depth), spot(d, yy, side)], load_sem.at[4 + n]))
                device, *columns = partner[side]
                w_sends.append(pltpu.make_async_remote_copy(
                    src_ref=w_hbm.at[mine, span(columns[d], yy, side)],
                    dst_ref=wx.at[side, theirs, spot(d, yy, side)],
                    send_sem=ws_sem.at[n], recv_sem=wr_sem.at[n],
                    device_id=device, device_id_type=MESH))

    def w_copy(n, rows):
        side, d, yy = n // 4, n // 2 % 2, n % 2
        block = wx.at[side, rows, spot(d, yy, side)]
        return pltpu.make_async_remote_copy(
            src_ref=block, dst_ref=block, send_sem=ws_sem.at[8 + n], recv_sem=wr_sem.at[8 + n],
            device_id=dev_sib, device_id_type=MESH)

    def pass_weights():
        for n in (0, 4, 1, 5, 2, 6, 3, 7):
            w_sends[n].wait_recv()
            w_copy(n, theirs).start()

    for load in loads:
        load.start()

    for d in range(1, SPAN):
        @pl.when(ctx < d)
        def _():
            kx[d, 0:ROWS, :] = jnp.zeros((ROWS, HD), jnp.bfloat16)
            kx[d, ROWS:, :] = jnp.full((SEGROWS, HD), -1.0, jnp.bfloat16)
            vv[d] = jnp.zeros((ROWS, HD), jnp.bfloat16)

    loads[0].wait()
    seg = seg_v[...].astype(jnp.float32)
    seg_lo, seg_hi = seg[:, :HD], seg[:, HD:]
    line = lax.broadcasted_iota(jnp.int32, (SEGROWS, HD), 0)
    both = jnp.where(line == 0, jnp.broadcast_to(seg_lo, (SEGROWS, HD)), jnp.broadcast_to(seg_hi, (SEGROWS, HD)))
    kx[0, ROWS:, :] = both.astype(jnp.bfloat16)
    first = jnp.min(seg, axis=1, keepdims=True)
    loads[1].wait()
    loads[2].wait()
    pl.semaphore_wait(barrier, 5 + core)

    def k_copy(index, slot, to_slot, device):
        return pltpu.make_async_remote_copy(
            src_ref=kx.at[slot], dst_ref=kx.at[to_slot],
            send_sem=ks_sem.at[index], recv_sem=kr_sem.at[to_slot],
            device_id=device, device_id_type=MESH)

    def v_copy(index, slot, to_slot, device):
        return pltpu.make_async_remote_copy(
            src_ref=vv.at[slot], dst_ref=vv.at[to_slot],
            send_sem=vs_sem.at[index], recv_sem=vr_sem.at[to_slot],
            device_id=device, device_id_type=MESH)

    plan = [
        (0, 2, dev_next, chip < chips - 1),
        (0, 1, dev_sib, core == 0),
        (2, 4, dev_next, (chip >= 1) & (chip < chips - 1)),
        (2, 3 - 2 * core, dev_sib, chip >= 1),
        (4, 5, (nxt * 2, head), (chip >= 2) & (chip < chips - 1) & (core == 1)),
        (4, 5 - 2 * core, dev_sib, chip >= 2),
    ]

    def send(make, slot, extra=True):
        for index, (source, target, device, cond) in enumerate(plan):
            if source == slot:
                @pl.when(cond & extra)
                def _():
                    make(index, source, target, device).start()

    def arrive(make, slot):
        @pl.when(ctx >= slot)
        def _():
            make(0, slot, slot, dev_next).wait_recv()

    send(k_copy, 0)
    send(v_copy, 0)
    for n in (0, 4, 1, 5, 2, 6, 3, 7):
        w_sends[n].start()
    loads[3].wait()

    scale = math.log2(math.e) / math.sqrt(HD)
    key_row = lax.broadcasted_iota(jnp.int32, (ROWS, ROWS), 0)
    count = share * (ROWS // LANES)
    peaks, totals = [None] * count, [None] * count

    def a_copy(side, n, rows, columns):
        return pltpu.make_async_remote_copy(
            src_ref=att.at[rows, columns], dst_ref=attx.at[side, rows, columns],
            send_sem=as_sem.at[side, n], recv_sem=ar_sem.at[side, n],
            device_id=partner[side][0], device_id_type=MESH)

    def a_copies(side, r):
        rows = pl.ds(*CHUNKS[r])
        if r == 0:
            return [a_copy(side, h, rows, pl.ds(h * HD, HD)) for h in range(share)]
        return [a_copy(side, share + r - 1, rows, pl.ds(0, share * HD))]

    def absorb(slot, allowed, place):
        vt = vv[slot].T
        for h in range(share):
            for half in range(ROWS // LANES):
                cols = slice(half * LANES, (half + 1) * LANES)
                n = h * (ROWS // LANES) + half
                scores = lax.dot_general(
                    kx[slot, 0:ROWS, :], q_v[cols, h * HD:(h + 1) * HD],
                    (((1,), (1,)), ((), ())), preferred_element_type=jnp.float32)
                scores = jnp.where(allowed[:, cols], scores, NEG)
                top = jnp.max(scores, axis=0, keepdims=True)
                if place > 0:
                    top = jnp.maximum(top, peaks[n])
                expo = jnp.exp2((scores - top) * scale)
                total = jnp.sum(expo, axis=0, keepdims=True)
                part = jnp.dot(vt, expo.astype(jnp.bfloat16), preferred_element_type=jnp.float32)
                if place > 0:
                    factor = jnp.exp2((peaks[n] - top) * scale)
                    total = total + totals[n] * factor
                    part = part + acc[h, :, cols] * factor
                peaks[n], totals[n] = top, total
                if place < SPAN - 1:
                    acc[h, :, cols] = part
                else:
                    att[cols, h * HD:(h + 1) * HD] = (part / total).T.astype(jnp.bfloat16)
            if place == SPAN - 1:
                for side in range(2):
                    a_copy(side, h, pl.ds(*CHUNKS[0]), pl.ds(h * HD, HD)).start()

    seg_col = jnp.concatenate(
        [jnp.broadcast_to(seg_lo, (HD, HD)).T, jnp.broadcast_to(seg_hi, (HD, HD)).T], axis=0)
    seg_col = jnp.concatenate([seg_col, seg_col], axis=1)
    query_col = lax.broadcasted_iota(jnp.int32, (ROWS, ROWS), 1)
    absorb(0, (seg_col == seg) & (key_row <= query_col), 0)
    order = ((2 - core, core == 0), (1 + core, core == 1), (4 - core, core == 0), (3 + core, core == 1), (5, None))
    for place, (slot, passes) in enumerate(order):
        source = (2, 2, 4, 4, 5)[place]
        for make in (k_copy, v_copy):
            arrive(make, slot)
            if passes is not None:
                send(make, source, passes)
        ids = kx[slot, ROWS:, :].astype(jnp.float32)
        same = jnp.where((line < 2) & (ids == first), 1.0, 0.0)
        count = jnp.sum(jnp.sum(same, axis=0, keepdims=True), axis=1, keepdims=True)
        start = jnp.where(seg == first, ROWS - count, float(ROWS)).astype(jnp.int32)
        absorb(slot, key_row >= start, place + 1)
        if place == 3:
            pl.when(chip % NZ < 2)(pass_weights)

    def exchange(r):
        for side in range(2):
            for copy in a_copies(side, r):
                copy.start()

    exchange(1)
    for load in loads[4:]:
        load.wait()
    pl.when(chip % NZ >= 2)(pass_weights)

    def s2_copy(side, r):
        rows = pl.ds(*CHUNKS[r])
        return pltpu.make_async_remote_copy(
            src_ref=s2.at[side, rows], dst_ref=r2.at[side, rows],
            send_sem=fs_sem.at[side, r], recv_sem=fr_sem.at[side, r],
            device_id=partner[1 - side][0], device_id_type=MESH)

    def s3_copy(r):
        rows = pl.ds(*CHUNKS[r])
        return pltpu.make_async_remote_copy(
            src_ref=s3.at[1 - yh, rows], dst_ref=r3.at[rows],
            send_sem=fs_sem.at[2, r], recv_sem=fr_sem.at[2, r],
            device_id=dev_y, device_id_type=MESH)

    def rows_of(r):
        return slice(CHUNKS[r][0], CHUNKS[r][0] + CHUNKS[r][1])

    def own_part(r):
        for side in range(2):
            own[side, rows_of(r)] = jnp.dot(
                att[rows_of(r)], wx[side, 0:depth], preferred_element_type=jnp.float32)

    def both_parts(r):
        for side in range(2):
            for copy in a_copies(side, r):
                copy.wait_recv()
            if r == 0:
                for n in range(side * 4, side * 4 + 4):
                    w_copy(n, others).wait_recv()
            both = own[side, rows_of(r)] + jnp.dot(
                attx[side, rows_of(r)], wx[side, depth:], preferred_element_type=jnp.float32)
            s2[side, rows_of(r)] = both[:, BLOCK:].astype(jnp.bfloat16)
            s2_copy(side, r).start()
            own[side, rows_of(r), 0:BLOCK] = both[:, :BLOCK]

    def hand_on(r):
        for side in range(2):
            s2_copy(side, r).wait_recv()
            both = own[side, rows_of(r), 0:BLOCK] + r2[side, rows_of(r)].astype(jnp.float32)
            for yy in range(2):
                first, width, place = PARTS[side][yy]
                res[yy, rows_of(r), first:first + width] = both[:, place:place + width]
                s3[yy, rows_of(r), first:first + width] = both[:, place:place + width].astype(jnp.bfloat16)
        s3_copy(r).start()

    own_part(0)
    for r in range(NCH):
        both_parts(r)
        if r + 2 < NCH:
            exchange(r + 2)
        if r + 1 < NCH:
            own_part(r + 1)
        if r >= 1:
            hand_on(r - 1)
    hand_on(NCH - 1)

    for r in range(NCH):
        s3_copy(r).wait_recv()
        out[rows_of(r)] = (res[yh, rows_of(r)] + r3[rows_of(r)].astype(jnp.float32)).astype(jnp.bfloat16)
    for r in range(NCH):
        s3_copy(r).wait_send()
        for side in range(2):
            s2_copy(side, r).wait_send()
            for copy in a_copies(side, r):
                copy.wait_send()
    for copy in w_sends:
        copy.wait_send()
    for n in range(8):
        w_copy(n, theirs).wait_send()
    for make in (k_copy, v_copy):
        for index, (source, target, device, cond) in enumerate(plan):
            @pl.when(cond)
            def _():
                make(index, source, target, device).wait_send()


def solution(mesh):
    chips = mesh.shape["ctx"] // 2

    def shards(queries, keys, values, segment_ids, out_weight):
        share = queries.shape[1] // HD
        cols = out_weight.shape[1] // mesh.shape["head"]
        bf, f32 = jnp.bfloat16, jnp.float32
        depth = out_weight.shape[0]
        return pl.pallas_call(
            functools.partial(kernel, chips, share),
            name="attend_project",
            out_shape=pltpu.VMEM((ROWS, cols), bf),
            in_specs=[pl.BlockSpec(memory_space=pl.ANY)] * 5,
            out_specs=pl.BlockSpec(memory_space=pltpu.VMEM),
            scratch_shapes=[
                pltpu.VMEM(queries.shape, bf),
                pltpu.VMEM((SPAN, ROWS + SEGROWS, HD), bf),
                pltpu.VMEM((SPAN, ROWS, HD), bf),
                pltpu.VMEM((1, ROWS), jnp.int32),
                pltpu.VMEM((2, 2 * depth, 2 * BLOCK), bf),
                pltpu.VMEM((share, HD, ROWS), f32),
                pltpu.VMEM(queries.shape, bf),
                pltpu.VMEM((2, *queries.shape), bf),
                pltpu.VMEM((2, ROWS, 2 * BLOCK), f32),
                pltpu.VMEM((2, ROWS, BLOCK), bf),
                pltpu.VMEM((2, ROWS, BLOCK), bf),
                pltpu.VMEM((2, ROWS, BLOCK), f32),
                pltpu.VMEM((2, ROWS, BLOCK), bf),
                pltpu.VMEM((ROWS, BLOCK), bf),
                pltpu.SemaphoreType.DMA((12,)),
                pltpu.SemaphoreType.DMA((SPAN,)),
                pltpu.SemaphoreType.DMA((SPAN,)),
                pltpu.SemaphoreType.DMA((SPAN,)),
                pltpu.SemaphoreType.DMA((SPAN,)),
                pltpu.SemaphoreType.DMA((16,)),
                pltpu.SemaphoreType.DMA((16,)),
                pltpu.SemaphoreType.DMA((2, share + NCH - 1)),
                pltpu.SemaphoreType.DMA((2, share + NCH - 1)),
                pltpu.SemaphoreType.DMA((3, NCH)),
                pltpu.SemaphoreType.DMA((3, NCH)),
            ],
            compiler_params=pltpu.CompilerParams(
                collective_id=0, has_side_effects=True, vmem_limit_bytes=60 * 2**20),
        )(queries, keys, values, segment_ids.reshape(1, ROWS), out_weight)

    in_specs = (P("ctx", "head"), P("ctx", "head"), P("ctx", "head"), P("ctx"), P("head", None))
    return jax.shard_map(shards, mesh=mesh, in_specs=in_specs, out_specs=P("ctx", "head"), check_vma=False)
```

time: 64.8 us -> 57.5 us (0.89)
  the two profiles are of different devices: /device:TPU:8 before, /device:TPU:64 now
where the time goes in v2:
time: 57.5 us; the launch traced here: 57.4 us
  Pallas kernels  56.7 us (99%)
  local copies, waits for them, and re-layouts  0.73 us (1%)
    pallas_call x1, Pallas kernels, shards(): pl.pallas_call(functools.partial(kernel, chips, share), name='attend_proj...  56.7 us

profile of v2, /device:TPU:64, one launch (start us, length us, event | category | flops | bytes accessed | tf_op | source)
XLA Modules:
  0.0 57.4 jit_solution(15067615417252214290)
XLA Ops:
  0.0 56.7 %attend_project.1 = bf16[256,640]{1,0:T(8,128)(2,1)S(1)} custom-call(bf16[256,640]{1,0:T(8,128)(2,1)} %q_hbm.1, bf16[256,128]{1,0:T(8,128)(2,1)} %k_hbm.1, bf16[256,128]{1,0:T(8,128)(2,1)} %v_hbm.1, s32[1,256]{1,0:T(1,128)} %bitcast.1, bf16[640,5120]{1,0:T(8,128)(2,1)} %w_hbm.1), custom_call_target="tpu_custom_call" | custom-call | tf_op jit(solution)/shard_map/attend_project/pallas_call | solution.py:322
  56.7 0.7 %copy.7 = bf16[256,640]{1,0:T(8,128)(2,1)} copy(bf16[256,640]{1,0:T(8,128)(2,1)S(1)} %attend_project.1) | data formatting | bytes 655360

commit v3 on v2

--- a/solution.py
+++ b/solution.py
@@ -26,7 +26,7 @@
 def kernel(
     chips, share,
     q_hbm, k_hbm, v_hbm, s_hbm, w_hbm, out,
-    q_v, kx, vv, seg_v, wx, acc, att, attx, own, s2, r2, res, s3, r3,
+    q_v, kx, vv, seg_v, wx, acc, probs, att, attx, own, s2, r2, res, s3, r3,
     load_sem, ks_sem, kr_sem, vs_sem, vr_sem, ws_sem, wr_sem, as_sem, ar_sem, fs_sem, fr_sem,
 ):
     ctx = lax.axis_index("ctx")
@@ -176,34 +176,53 @@
             return [a_copy(side, h, rows, pl.ds(h * HD, HD)) for h in range(share)]
         return [a_copy(side, share + r - 1, rows, pl.ds(0, share * HD))]
 
+    def exchange(r):
+        for side in range(2):
+            for copy in a_copies(side, r):
+                copy.start()
+
+    tiles = [(h, half) for half in range(ROWS // LANES) for h in range(share)]
+
     def absorb(slot, allowed, place):
+        last = place == SPAN - 1
+        vt = None if last else vv[slot].T
+        factors = [None] * len(tiles)
+        for n, (h, half) in enumerate(tiles):
+            cols = slice(half * LANES, (half + 1) * LANES)
+            scores = lax.dot_general(
+                kx[slot, 0:ROWS, :], q_v[cols, h * HD:(h + 1) * HD],
+                (((1,), (1,)), ((), ())), preferred_element_type=jnp.float32)
+            scores = jnp.where(allowed[:, cols], scores, NEG)
+            top = jnp.max(scores, axis=0, keepdims=True)
+            if place > 0:
+                top = jnp.maximum(top, peaks[n])
+            expo = jnp.exp2((scores - top) * scale)
+            total = jnp.sum(expo, axis=0, keepdims=True)
+            if place > 0:
+                factors[n] = jnp.exp2((peaks[n] - top) * scale)
+                total = total + totals[n] * factors[n]
+            peaks[n], totals[n] = top, total
+            if last:
+                probs[n] = expo.astype(jnp.bfloat16)
+                continue
+            part = jnp.dot(vt, expo.astype(jnp.bfloat16), preferred_element_type=jnp.float32)
+            if place > 0:
+                part = part + acc[h, :, cols] * factors[n]
+            acc[h, :, cols] = part
+        if not last:
+            return
+        arrive(v_copy, slot)
         vt = vv[slot].T
-        for h in range(share):
-            for half in range(ROWS // LANES):
-                cols = slice(half * LANES, (half + 1) * LANES)
-                n = h * (ROWS // LANES) + half
-                scores = lax.dot_general(
-                    kx[slot, 0:ROWS, :], q_v[cols, h * HD:(h + 1) * HD],
-                    (((1,), (1,)), ((), ())), preferred_element_type=jnp.float32)
-                scores = jnp.where(allowed[:, cols], scores, NEG)
-                top = jnp.max(scores, axis=0, keepdims=True)
-                if place > 0:
-                    top = jnp.maximum(top, peaks[n])
-                expo = jnp.exp2((scores - top) * scale)
-                total = jnp.sum(expo, axis=0, keepdims=True)
-                part = jnp.dot(vt, expo.astype(jnp.bfloat16), preferred_element_type=jnp.float32)
-                if place > 0:
-                    factor = jnp.exp2((peaks[n] - top) * scale)
-                    total = total + totals[n] * factor
-                    part = part + acc[h, :, cols] * factor
-                peaks[n], totals[n] = top, total
-                if place < SPAN - 1:
-                    acc[h, :, cols] = part
-                else:
-                    att[cols, h * HD:(h + 1) * HD] = (part / total).T.astype(jnp.bfloat16)
-            if place == SPAN - 1:
+        for n, (h, half) in enumerate(tiles):
+            cols = slice(half * LANES, (half + 1) * LANES)
+            part = jnp.dot(vt, probs[n], preferred_element_type=jnp.float32)
+            part = (part + acc[h, :, cols] * factors[n]) / totals[n]
+            att[cols, h * HD:(h + 1) * HD] = part.T.astype(jnp.bfloat16)
+            if half == 0:
                 for side in range(2):
                     a_copy(side, h, pl.ds(*CHUNKS[0]), pl.ds(h * HD, HD)).start()
+                if h == share - 1:
+                    exchange(1)
 
     seg_col = jnp.concatenate(
         [jnp.broadcast_to(seg_lo, (HD, HD)).T, jnp.broadcast_to(seg_hi, (HD, HD)).T], axis=0)
@@ -213,7 +232,7 @@
     order = ((2 - core, core == 0), (1 + core, core == 1), (4 - core, core == 0), (3 + core, core == 1), (5, None))
     for place, (slot, passes) in enumerate(order):
         source = (2, 2, 4, 4, 5)[place]
-        for make in (k_copy, v_copy):
+        for make in (k_copy, v_copy) if place < SPAN - 2 else (k_copy,):
             arrive(make, slot)
             if passes is not None:
                 send(make, source, passes)
@@ -225,12 +244,6 @@
         if place == 3:
             pl.when(chip % NZ < 2)(pass_weights)
 
-    def exchange(r):
-        for side in range(2):
-            for copy in a_copies(side, r):
-                copy.start()
-
-    exchange(1)
     for load in loads[4:]:
         load.wait()
     pl.when(chip % NZ >= 2)(pass_weights)
@@ -252,10 +265,9 @@
     def rows_of(r):
         return slice(CHUNKS[r][0], CHUNKS[r][0] + CHUNKS[r][1])
 
-    def own_part(r):
-        for side in range(2):
-            own[side, rows_of(r)] = jnp.dot(
-                att[rows_of(r)], wx[side, 0:depth], preferred_element_type=jnp.float32)
+    def own_part():
+        for side in range(2):
+            own[side] = jnp.dot(att[...], wx[side, 0:depth], preferred_element_type=jnp.float32)
 
     def both_parts(r):
         for side in range(2):
@@ -280,13 +292,11 @@
                 s3[yy, rows_of(r), first:first + width] = both[:, place:place + width].astype(jnp.bfloat16)
         s3_copy(r).start()
 
-    own_part(0)
+    own_part()
     for r in range(NCH):
         both_parts(r)
         if r + 2 < NCH:
             exchange(r + 2)
-        if r + 1 < NCH:
-            own_part(r + 1)
         if r >= 1:
             hand_on(r - 1)
     hand_on(NCH - 1)
@@ -332,6 +342,7 @@
                 pltpu.VMEM((1, ROWS), jnp.int32),
                 pltpu.VMEM((2, 2 * depth, 2 * BLOCK), bf),
                 pltpu.VMEM((share, HD, ROWS), f32),
+                pltpu.VMEM((share * (ROWS // LANES), ROWS, LANES), bf),
                 pltpu.VMEM(queries.shape, bf),
                 pltpu.VMEM((2, *queries.shape), bf),
                 pltpu.VMEM((2, ROWS, 2 * BLOCK), f32),

time: 57.5 us -> 56 us (0.974)
  the two profiles are of different devices: /device:TPU:64 before, /device:TPU:1 now
where the time goes in v3:
time: 56 us; the launch traced here: 55.8 us
  Pallas kernels  55.1 us (98%)
  local copies, waits for them, and re-layouts  0.73 us (1%)
    pallas_call x1, Pallas kernels, shards(): pl.pallas_call(functools.partial(kernel, chips, share), name='attend_proj...  55.1 us

profile of v3, /device:TPU:1, one launch (start us, length us, event | category | flops | bytes accessed | tf_op | source)
XLA Modules:
  0.0 55.8 jit_solution(9604089070670026204)
XLA Ops:
  0.0 55.1 %attend_project.1 = bf16[256,640]{1,0:T(8,128)(2,1)S(1)} custom-call(bf16[256,640]{1,0:T(8,128)(2,1)} %q_hbm.1, bf16[256,128]{1,0:T(8,128)(2,1)} %k_hbm.1, bf16[256,128]{1,0:T(8,128)(2,1)} %v_hbm.1, s32[1,256]{1,0:T(1,128)} %bitcast.1, bf16[640,5120]{1,0:T(8,128)(2,1)} %w_hbm.1), custom_call_target="tpu_custom_call" | custom-call | tf_op jit(solution)/shard_map/attend_project/pallas_call | solution.py:332
  55.1 0.7 %copy.7 = bf16[256,640]{1,0:T(8,128)(2,1)} copy(bf16[256,640]{1,0:T(8,128)(2,1)S(1)} %attend_project.1) | data formatting | bytes 655360

commit v4 on v3

--- a/solution.py
+++ b/solution.py
@@ -155,8 +155,11 @@
 
     send(k_copy, 0)
     send(v_copy, 0)
-    for n in (0, 4, 1, 5, 2, 6, 3, 7):
-        w_sends[n].start()
+    def send_weights():
+        for n in (0, 4, 1, 5, 2, 6, 3, 7):
+            w_sends[n].start()
+
+    pl.when(chip % NZ < 9)(send_weights)
     loads[3].wait()
 
     scale = math.log2(math.e) / math.sqrt(HD)
@@ -241,6 +244,8 @@
         count = jnp.sum(jnp.sum(same, axis=0, keepdims=True), axis=1, keepdims=True)
         start = jnp.where(seg == first, ROWS - count, float(ROWS)).astype(jnp.int32)
         absorb(slot, key_row >= start, place + 1)
+        if place == 1:
+            pl.when(chip % NZ >= 9)(send_weights)
         if place == 3:
             pl.when(chip % NZ < 2)(pass_weights)
 

time: 56 us -> 58.4 us (1.043)
  the two profiles are of different devices: /device:TPU:1 before, /device:TPU:642 now
where the time goes in v4:
time: 58.4 us; the launch traced here: 58.3 us
  Pallas kernels  57.6 us (99%)
  local copies, waits for them, and re-layouts  0.73 us (1%)
    pallas_call x1, Pallas kernels, shards(): pl.pallas_call(functools.partial(kernel, chips, share), name='attend_proj...  57.6 us

profile of v4, /device:TPU:642, one launch (start us, length us, event | category | flops | bytes accessed | tf_op | source)
XLA Modules:
  0.0 58.3 jit_solution(11265603961426655640)
XLA Ops:
  0.0 57.6 %attend_project.1 = bf16[256,640]{1,0:T(8,128)(2,1)S(1)} custom-call(bf16[256,640]{1,0:T(8,128)(2,1)} %q_hbm.1, bf16[256,128]{1,0:T(8,128)(2,1)} %k_hbm.1, bf16[256,128]{1,0:T(8,128)(2,1)} %v_hbm.1, s32[1,256]{1,0:T(1,128)} %bitcast.1, bf16[640,5120]{1,0:T(8,128)(2,1)} %w_hbm.1), custom_call_target="tpu_custom_call" | custom-call | tf_op jit(solution)/shard_map/attend_project/pallas_call | solution.py:337
  57.6 0.7 %copy.7 = bf16[256,640]{1,0:T(8,128)(2,1)} copy(bf16[256,640]{1,0:T(8,128)(2,1)S(1)} %attend_project.1) | data formatting | bytes 655360
